TPU v7x, 32 devices: a whole 2x2x4 slice. The times are simulated.
32 devices in a mesh: beam: 4 (over y, x), chan: 8 (over z, core).
Axes of the slice: x: 2, y: 2, z: 4, core: 2. Of those that a mesh axis runs over, the one named last changes fastest.
Arguments:
- intensities: bfloat16 [32, 8192, 128], P(None, ('beam', 'chan')), may hold values from -6 to 6
- lower_index: int32 [10, 1024], replicated, may hold values from 0 to 511, as said below
- upper_index: int32 [10, 1024], replicated, may hold values from 0 to 511, as said below
- delay_shift: int32 [10, 1024], replicated, may hold values from 0 to 512, as said below
- widths: int32 [8], replicated, may hold values from 1 to 64, as said below
- max_delay: int32 [32], P(('beam', 'chan')), may hold values from 256 to 1023
Outputs:
- snr: float32 [32, 8, 1024], P(('beam', 'chan'))
Inputs may be any that keep to these rules, and one draw needn't show every extreme that they name: `lower_index`: at level l and row r, with d = r mod 2^(l+1), the entry is either floor(d / 2) or min(floor((d + 1) / 2), 2^l - 1). `upper_index`: at level l and row r, with d = r mod 2^(l+1), the entry is either floor(d / 2) or min(floor((d + 1) / 2), 2^l - 1). `delay_shift`: at level l the shift is at most 2^l. Distinct widths; 1 and 64 are always among them.
All inputs are finite; a program needn't handle non-finite values.
Results may differ from a plain program's by a relative error of at most 0.0003.
Values sent between devices are 32-bit elements; how exact they have to be, the bound alone decides.
A program may use at most 64 MiB of HBM per device.

v0:
```python
import functools

import jax
import jax.numpy as jnp
from jax import lax
from jax.experimental import pallas as pl
from jax.experimental.pallas import tpu as pltpu
from jax.sharding import PartitionSpec as P

SUB0 = 8
ROWS = 8
MESH = pl.DeviceIdType.MESH


def xor(left, right, size):
    total = 0
    for bit in range(size.bit_length() - 1):
        step = 1 << bit
        total = total + step * ((left // step + right // step) % 2)
    return total


def take(values, index, axis):
    return jnp.take_along_axis(values, index, axis=axis, mode="promise_in_bounds")


def build_indices(levels, bands, samples, lower_ref, upper_ref, shift_ref, low_at, up_at, time_at):
    depth = 16
    zeros = jnp.zeros((depth - levels, bands), jnp.int32)
    lower = jnp.concatenate([lower_ref[...], zeros], axis=0)
    upper = jnp.concatenate([upper_ref[...], zeros], axis=0)
    shift = jnp.concatenate([shift_ref[...], zeros], axis=0)
    level = lax.broadcasted_iota(jnp.int32, (depth, bands), 0)
    row = lax.broadcasted_iota(jnp.int32, (depth, bands), 1)
    width = jnp.left_shift(jnp.int32(2), level)
    trial = row & (width - 1)
    inside = (row & (ROWS - 1)) - trial
    skip = jnp.where(level >= 4, 4 * (trial // ROWS), 0)
    lower = jnp.where(level <= 2, inside + lower, lower - skip) & (ROWS - 1)
    upper = jnp.where(level <= 2, inside + width // 2 + upper, upper - skip) & (ROWS - 1)
    packed = jnp.concatenate(
        [(lower + ROWS * upper).astype(jnp.float32), jnp.minimum(shift, samples).astype(jnp.float32)],
        axis=0,
    ).astype(jnp.bfloat16)
    entry = lax.broadcasted_iota(jnp.int32, (2 * depth, samples), 0)
    time = lax.broadcasted_iota(jnp.int32, (bands, samples), 1)
    for step in range(levels):
        spread = jnp.where(entry == step, 256.0, jnp.where(entry == depth + step, 1.0, 0.0))
        value = lax.dot_general(
            packed,
            spread.astype(jnp.bfloat16),
            (((0,), (0,)), ((), ())),
            preferred_element_type=jnp.float32,
        ).astype(jnp.int32)
        low_at[step] = (value >> 8) & (ROWS - 1)
        up_at[step] = value >> 11
        time_at[step] = time - (value & 255)


def merge(lower, upper, step, rows, low_at, up_at, time_at):
    samples = lower.shape[-1]
    when = time_at[step, rows]
    upper = take(upper, up_at[step, rows], 0)
    upper = take(upper, when & (samples - 1), 1)
    return take(lower, low_at[step, rows], 0) + jnp.where(when >= 0, upper, 0.0)


def first_levels(block, start, rows_each, got, out, low_at, up_at, time_at):
    for piece in range(rows_each // ROWS):
        rows = pl.ds(pl.multiple_of(start + piece * ROWS, ROWS), ROWS)
        value = got[block, pl.ds(piece * ROWS, ROWS)]
        for step in range(3):
            value = merge(value, value, step, rows, low_at, up_at, time_at)
        out[rows] = value


def pair_rows(pair, step, source, out, low_at, up_at, time_at):
    width = 2 << step
    start = pl.multiple_of(pair * 2 * ROWS, 2 * ROWS)
    trial = start % width
    base = start - trial
    low_row = pl.multiple_of(base + trial // 2, ROWS)
    up_row = pl.multiple_of(base + width // 2 + trial // 2, ROWS)
    for odd in range(2):
        rows = pl.ds(start + odd * ROWS, ROWS)
        move = 4 * odd if step >= 4 else 0
        lower = source[pl.ds(low_row + move, ROWS)]
        upper = source[pl.ds(up_row + move, ROWS)]
        out[rows] = merge(lower, upper, step, rows, low_at, up_at, time_at)


def scores(trials_ref, widths_ref, limit_ref, out_ref, bands, samples, chunk):
    boxes = out_ref.shape[1]
    source = lax.broadcasted_iota(jnp.int32, (samples, 2 * samples), 1) % samples
    target = lax.broadcasted_iota(jnp.int32, (samples, 2 * samples), 0)
    limit = limit_ref[0]
    kernels = []
    for box in range(boxes):
        width = widths_ref[box]
        back = target - source
        hit = jnp.where((back >= 0) & (back < width), 1.0, 0.0)
        mean = jnp.minimum(width, samples - source).astype(jnp.float32) * (1.0 / samples)
        kernels.append((hit - mean).astype(jnp.bfloat16))
    for part in range(bands // chunk):
        trials = trials_ref[pl.ds(part * chunk, chunk)]
        high = trials.astype(jnp.bfloat16)
        low = (trials - high.astype(jnp.float32)).astype(jnp.bfloat16)
        both = jnp.concatenate([high, low], axis=1)
        keep = lax.broadcasted_iota(jnp.int32, (1, chunk), 1) + part * chunk <= limit
        for box in range(boxes):
            offset = lax.dot_general(
                kernels[box], both, (((1,), (1,)), ((), ())), preferred_element_type=jnp.float32
            )
            top = jnp.max(offset, axis=0, keepdims=True)
            spread = jnp.sum(offset * offset, axis=0, keepdims=True) * (1.0 / samples)
            value = jnp.where(keep, top / jnp.sqrt(spread + 1e-05), 0.0)
            out_ref[0, pl.ds(box, 1), pl.ds(part * chunk, chunk)] = value


def kernel(
    beam_count, chan_count,
    x_ref, lower_ref, upper_ref, shift_ref, widths_ref, limit_ref, out_ref,
    sums, got, ping, pong, low_at, up_at, time_at, send_sem, recv_sem,
):
    count = beam_count * chan_count
    beam, chan = lax.axis_index("beam"), lax.axis_index("chan")
    me = beam * chan_count + chan
    channels, samples = x_ref.shape[1], x_ref.shape[2]
    rows_each = channels // SUB0
    bands = count * rows_each
    levels = bands.bit_length() - 1

    def partner(turn):
        chan_to = xor(chan, chan_count - 1 - turn // beam_count, chan_count)
        beam_to = xor(beam, beam_count - 1 - turn % beam_count, beam_count)
        return beam_to, chan_to

    barrier = pltpu.get_barrier_semaphore()

    def greet(turn, carry):
        pl.semaphore_signal(barrier, inc=1, device_id=partner(turn), device_id_type=MESH)
        return carry

    lax.fori_loop(0, count - 1, greet, 0)
    band = lax.broadcasted_iota(jnp.int32, (rows_each, channels), 0)
    channel = lax.broadcasted_iota(jnp.int32, (rows_each, channels), 1)
    adder = jnp.where(channel // SUB0 == band, 1.0, 0.0).astype(jnp.bfloat16)
    pl.semaphore_wait(barrier, count - 1)

    def copy_of(turn):
        return pltpu.make_async_remote_copy(
            src_ref=sums.at[turn],
            dst_ref=got.at[me],
            send_sem=send_sem.at[turn],
            recv_sem=recv_sem.at[turn],
            device_id=partner(turn),
            device_id_type=MESH,
        )

    def send(turn, carry):
        beam_to, chan_to = partner(turn)
        sums[turn] = jnp.dot(
            adder, x_ref[beam_to * chan_count + chan_to], preferred_element_type=jnp.float32
        )
        copy_of(turn).start()
        return carry

    lax.fori_loop(0, count - 1, send, 0)
    got[me] = jnp.dot(adder, x_ref[me], preferred_element_type=jnp.float32)
    build_indices(levels, bands, samples, lower_ref, upper_ref, shift_ref, low_at, up_at, time_at)
    ping[pl.ds(bands, ROWS)] = jnp.zeros((ROWS, samples), jnp.float32)
    pong[pl.ds(bands, ROWS)] = jnp.zeros((ROWS, samples), jnp.float32)

    def finish(turn, carry):
        copy_of(turn).wait()
        return carry

    lax.fori_loop(0, count - 1, finish, 0)

    def first(block, carry):
        first_levels(
            block, block * rows_each, rows_each, got, ping, low_at, up_at, time_at
        )
        return carry

    lax.fori_loop(0, count, first, 0)
    source, out = ping, pong
    for step in range(3, levels):
        def pairs(group, carry):
            for inner in range(4):
                pair_rows(4 * group + inner, step, source, out, low_at, up_at, time_at)
            return carry
        lax.fori_loop(0, bands // (8 * ROWS), pairs, 0)
        source, out = out, source
    scores(source, widths_ref, limit_ref, out_ref, bands, samples, 256)


def shards(intensities, lower_index, upper_index, delay_shift, widths, max_delay):
    beam_count = lax.axis_size("beam")
    chan_count = lax.axis_size("chan")
    count = beam_count * chan_count
    beams, channels, samples = intensities.shape
    rows_each = channels // SUB0
    bands = count * rows_each
    levels = lower_index.shape[0]
    vmem = pl.BlockSpec(memory_space=pltpu.VMEM)
    smem = pl.BlockSpec(memory_space=pltpu.SMEM)
    return pl.pallas_call(
        functools.partial(kernel, beam_count, chan_count),
        out_shape=jax.ShapeDtypeStruct((1, widths.shape[0], bands), jnp.float32),
        in_specs=[vmem] * 4 + [smem] * 2,
        out_specs=vmem,
        scratch_shapes=[
            pltpu.VMEM((count, rows_each, samples), jnp.float32),
            pltpu.VMEM((count, rows_each, samples), jnp.float32),
            pltpu.VMEM((bands + ROWS, samples), jnp.float32),
            pltpu.VMEM((bands + ROWS, samples), jnp.float32),
            pltpu.VMEM((levels, bands, samples), jnp.int32),
            pltpu.VMEM((levels, bands, samples), jnp.int32),
            pltpu.VMEM((levels, bands, samples), jnp.int32),
            pltpu.SemaphoreType.DMA((count,)),
            pltpu.SemaphoreType.DMA((count,)),
        ],
        compiler_params=pltpu.CompilerParams(
            collective_id=0, has_side_effects=True, vmem_limit_bytes=48 * 1024 * 1024
        ),
        name="search",
    )(intensities, lower_index, upper_index, delay_shift, widths, max_delay)


def solution(mesh):
    in_specs = (P(None, ("beam", "chan"), None), P(), P(), P(), P(), P(("beam", "chan")))
    out_specs = P(("beam", "chan"), None, None)
    return jax.shard_map(shards, mesh=mesh, in_specs=in_specs, out_specs=out_specs, check_vma=False)
```

profile of v0, /device:TPU:0, one launch (start us, length us, event | category | flops | bytes accessed | tf_op | source)
XLA Modules:
  0.0 48.7 jit_solution(12648356019956680575)
XLA Ops:
  0.7 0.0 copy-start
  0.7 1.6 %copy-done = bf16[32,256,128]{2,1,0:T(8,128)(2,1)S(1)} copy-done((bf16[32,256,128]{2,1,0:T(8,128)(2,1)S(1)}, bf16[32,256,128]{2,1,0:T(8,128)(2,1)}, u32[]{:S(2)}) %copy-start) | copy-done | bytes 2097176
  2.2 0.0 copy-start.1
  2.2 0.8 %copy-done.1 = s32[10,1024]{1,0:T(8,128)S(1)} copy-done((s32[10,1024]{1,0:T(8,128)S(1)}, s32[10,1024]{1,0:T(8,128)}, u32[]{:S(2)}) %copy-start.1) | copy-done | bytes 40984
  3.1 0.0 copy-start.2
  3.1 0.8 %copy-done.2 = s32[10,1024]{1,0:T(8,128)S(1)} copy-done((s32[10,1024]{1,0:T(8,128)S(1)}, s32[10,1024]{1,0:T(8,128)}, u32[]{:S(2)}) %copy-start.2) | copy-done | bytes 40984
  3.9 0.0 copy-start.3
  3.9 0.8 %copy-done.3 = s32[10,1024]{1,0:T(8,128)S(1)} copy-done((s32[10,1024]{1,0:T(8,128)S(1)}, s32[10,1024]{1,0:T(8,128)}, u32[]{:S(2)}) %copy-start.3) | copy-done | bytes 40984
  4.8 0.0 copy-start.4
  4.8 0.7 %copy-done.4 = s32[8]{0:T(128)S(1)} copy-done((s32[8]{0:T(128)S(1)}, s32[8]{0:T(128)}, u32[]{:S(2)}) %copy-start.4) | copy-done | bytes 56
  5.4 42.7 %search.1 = f32[1,8,1024]{2,1,0:T(8,128)S(1)} custom-call(bf16[32,256,128]{2,1,0:T(8,128)(2,1)S(1)} %copy-done, s32[10,1024]{1,0:T(8,128)S(1)} %copy-done.1, s32[10,1024]{1,0:T(8,128)S(1)} %copy-done.2, s32[10,1024]{1,0:T(8,128)S(1)} %copy-done.3, s32[8]{0:T(128)S(1)} %copy-done.4, s32[1]{0:T(128)S(6)} %copy.8.limit_ref), custom_call_target="tpu_custom_call" | custom-call | tf_op jit(solution)/shard_map/search/pallas_call | solution.py:208
  48.1 0.6 %copy.9 = f32[1,8,1024]{2,1,0:T(8,128)} copy(f32[1,8,1024]{2,1,0:T(8,128)S(1)} %search.1) | data formatting | bytes 65536
Async XLA Ops:
  0.7 1.6 %copy-start = (bf16[32,256,128]{2,1,0:T(8,128)(2,1)S(1)}, bf16[32,256,128]{2,1,0:T(8,128)(2,1)}, u32[]{:S(2)}) copy-start(bf16[32,256,128]{2,1,0:T(8,128)(2,1)} %x_ref.1) | copy-start | bytes 6291460
  2.2 0.8 %copy-start.1 = (s32[10,1024]{1,0:T(8,128)S(1)}, s32[10,1024]{1,0:T(8,128)}, u32[]{:S(2)}) copy-start(s32[10,1024]{1,0:T(8,128)} %lower_ref.1) | copy-start | bytes 122884
  3.1 0.8 %copy-start.2 = (s32[10,1024]{1,0:T(8,128)S(1)}, s32[10,1024]{1,0:T(8,128)}, u32[]{:S(2)}) copy-start(s32[10,1024]{1,0:T(8,128)} %upper_ref.1) | copy-start | bytes 122884
  3.9 0.8 %copy-start.3 = (s32[10,1024]{1,0:T(8,128)S(1)}, s32[10,1024]{1,0:T(8,128)}, u32[]{:S(2)}) copy-start(s32[10,1024]{1,0:T(8,128)} %shift_ref.1) | copy-start | bytes 122884
  4.8 0.7 %copy-start.4 = (s32[8]{0:T(128)S(1)}, s32[8]{0:T(128)}, u32[]{:S(2)}) copy-start(s32[8]{0:T(128)} %widths_ref.1) | copy-start | bytes 100
where the time goes:
time: 49 us; the launch traced here: 48.7 us
  Pallas kernels  42.7 us (87%)
  local copies, waits for them, and re-layouts  5.37 us (11%)
  between operations  0.67 us (1%)
    pallas_call x1, Pallas kernels, shards(): pl.pallas_call(functools.partial(kernel, beam_count, chan_count), out_sha...  42.7 us
    unnamed x11, local copies, waits for them, and re-layouts  5.37 us

commit v1 on v0

v1 whole, which is shorter than its diff:
```python
import functools

import jax
import jax.numpy as jnp
from jax import lax
from jax.experimental import pallas as pl
from jax.experimental.pallas import tpu as pltpu
from jax.sharding import PartitionSpec as P

SUB0 = 8
ROWS = 8
BATCH = 16
CHUNKS = 4
MESH = pl.DeviceIdType.MESH


def take(values, index, axis):
    return jnp.take_along_axis(values, index, axis=axis, mode="promise_in_bounds")


def build_indices(levels, bands, samples, lower_ref, upper_ref, shift_ref, low_at, up_at, time_at):
    depth = 16
    zeros = jnp.zeros((depth - levels, bands), jnp.int32)
    lower = jnp.concatenate([lower_ref[...], zeros], axis=0)
    upper = jnp.concatenate([upper_ref[...], zeros], axis=0)
    shift = jnp.concatenate([shift_ref[...], zeros], axis=0)
    level = lax.broadcasted_iota(jnp.int32, (depth, bands), 0)
    row = lax.broadcasted_iota(jnp.int32, (depth, bands), 1)
    width = jnp.left_shift(jnp.int32(2), level)
    trial = row & (width - 1)
    inside = (row & (ROWS - 1)) - trial
    skip = jnp.where(level >= 4, 4 * (trial // ROWS), 0)
    lower = jnp.where(level <= 2, inside + lower, lower - skip) & (ROWS - 1)
    upper = jnp.where(level <= 2, inside + width // 2 + upper, upper - skip) & (ROWS - 1)
    packed = jnp.concatenate(
        [(lower + ROWS * upper).astype(jnp.float32), jnp.minimum(shift, samples).astype(jnp.float32)],
        axis=0,
    ).astype(jnp.bfloat16)
    entry = lax.broadcasted_iota(jnp.int32, (2 * depth, samples), 0)
    time = lax.broadcasted_iota(jnp.int32, (bands, samples), 1)
    for step in range(levels):
        spread = jnp.where(entry == step, 256.0, jnp.where(entry == depth + step, 1.0, 0.0))
        value = lax.dot_general(
            packed,
            spread.astype(jnp.bfloat16),
            (((0,), (0,)), ((), ())),
            preferred_element_type=jnp.float32,
        ).astype(jnp.int32)
        low_at[step] = (value >> 8) & (ROWS - 1)
        up_at[step] = value >> 11
        time_at[step] = time - (value & 255)


def merge_rows(step, places, source, out, low_at, up_at, time_at):
    samples = out.shape[-1]
    for at in range(0, len(places), BATCH):
        batch = places[at : at + BATCH]
        outs = [pl.ds(row, ROWS) for row, _, _ in batch]
        lowers = [source[pl.ds(row, ROWS)] for _, row, _ in batch]
        uppers = [source[pl.ds(row, ROWS)] for _, _, row in batch]
        whens = [time_at[step, rows] for rows in outs]
        uppers = [take(v, up_at[step, rows], 0) for v, rows in zip(uppers, outs)]
        lowers = [take(v, low_at[step, rows], 0) for v, rows in zip(lowers, outs)]
        uppers = [take(v, when & (samples - 1), 1) for v, when in zip(uppers, whens)]
        for rows, lower, upper, when in zip(outs, lowers, uppers, whens):
            out[rows] = lower + jnp.where(when >= 0, upper, 0.0)


def places_of(step, start, size):
    width = 2 << step
    places = []
    for offset in range(0, size, ROWS):
        row = start + offset
        if width <= ROWS:
            places.append((row, row, row))
            continue
        trial = offset % width
        skip = 4 * (trial // ROWS) if step >= 4 else 0
        base = offset - trial
        places.append((row, start + base + skip, start + base + width // 2 + skip))
    return places


def scores(trials_ref, widths_ref, limit_ref, out_ref, bands, samples, chunk):
    boxes = out_ref.shape[1]
    source = lax.broadcasted_iota(jnp.int32, (samples, 2 * samples), 1) % samples
    target = lax.broadcasted_iota(jnp.int32, (samples, 2 * samples), 0)
    limit = limit_ref[0]
    kernels = []
    for box in range(boxes):
        width = widths_ref[box]
        back = target - source
        hit = jnp.where((back >= 0) & (back < width), 1.0, 0.0)
        mean = jnp.minimum(width, samples - source).astype(jnp.float32) * (1.0 / samples)
        kernels.append((hit - mean).astype(jnp.bfloat16))
    for part in range(bands // chunk):
        trials = trials_ref[pl.ds(part * chunk, chunk)]
        high = trials.astype(jnp.bfloat16)
        low = (trials - high.astype(jnp.float32)).astype(jnp.bfloat16)
        both = jnp.concatenate([high, low], axis=1)
        keep = lax.broadcasted_iota(jnp.int32, (1, chunk), 1) + part * chunk <= limit
        for box in range(boxes):
            offset = lax.dot_general(
                kernels[box], both, (((1,), (1,)), ((), ())), preferred_element_type=jnp.float32
            )
            top = jnp.max(offset, axis=0, keepdims=True)
            spread = jnp.sum(offset * offset, axis=0, keepdims=True) * (1.0 / samples)
            value = jnp.where(keep, top / jnp.sqrt(spread + 1e-05), 0.0)
            out_ref[0, pl.ds(box, 1), pl.ds(part * chunk, chunk)] = value


def kernel(
    beam_count, chan_count, levels,
    x_hbm, lower_hbm, upper_hbm, shift_hbm, widths_hbm, limit_hbm, out_ref,
    x_ref, lower_ref, upper_ref, shift_ref, widths_ref, limit_ref, sums, got, *rest,
):
    states, (low_at, up_at, time_at, load_sem, send_sem, recv_sem) = rest[:levels], rest[levels:]
    count = beam_count * chan_count
    beam, chan = lax.axis_index("beam"), lax.axis_index("chan")
    me = beam * chan_count + chan
    channels, samples = x_ref.shape[1], x_ref.shape[2]
    rows_each = channels // SUB0
    bands = count * rows_each
    beams_each = count // CHUNKS

    def flips(value, size):
        return [(1 << bit) * (1 - 2 * (value // (1 << bit) % 2)) for bit in range(size.bit_length() - 1)]

    beam_flips, chan_flips = flips(beam, beam_count), flips(chan, chan_count)

    def xor(value, steps, mask):
        for bit, step in enumerate(steps):
            if mask >> bit & 1:
                value = value + step
        return value

    turns = [(c, b) for c in reversed(range(chan_count)) for b in range(beam_count) if (c, b) != (0, 0)]

    def partner(c, b):
        return xor(beam, beam_flips, b), xor(chan, chan_flips, c)

    barrier = pltpu.get_barrier_semaphore()
    loads = [
        pltpu.make_async_copy(
            x_hbm.at[pl.ds(part * beams_each, beams_each)],
            x_ref.at[pl.ds(part * beams_each, beams_each)],
            load_sem.at[part],
        )
        for part in range(CHUNKS)
    ]
    others = [(lower_hbm, lower_ref), (upper_hbm, upper_ref), (shift_hbm, shift_ref), (widths_hbm, widths_ref), (limit_hbm, limit_ref)]
    tables = [
        pltpu.make_async_copy(source, target, load_sem.at[CHUNKS + at])
        for at, (source, target) in enumerate(others)
    ]
    for load in loads + tables:
        load.start()
    for c, b in turns:
        pl.semaphore_signal(barrier, inc=1, device_id=partner(c, b), device_id_type=MESH)

    band = lax.broadcasted_iota(jnp.int32, (rows_each, channels), 0)
    channel = lax.broadcasted_iota(jnp.int32, (rows_each, channels), 1)
    adder = jnp.where(channel // SUB0 == band, 1.0, 0.0).astype(jnp.bfloat16)
    for part, load in enumerate(loads):
        load.wait()
        for owner in range(part * beams_each, (part + 1) * beams_each):
            sums[owner] = jnp.dot(adder, x_ref[owner], preferred_element_type=jnp.float32)
    for load in tables:
        load.wait()
    pl.semaphore_wait(barrier, count - 1)

    copies = {}
    for c, b in turns:
        beam_to, chan_to = partner(c, b)
        copies[c, b] = pltpu.make_async_remote_copy(
            src_ref=sums.at[beam_to * chan_count + chan_to],
            dst_ref=got.at[me],
            send_sem=send_sem.at[c * beam_count + b],
            recv_sem=recv_sem.at[c * beam_count + b],
            device_id=(beam_to, chan_to),
            device_id_type=MESH,
        )
        copies[c, b].start()
    got[me] = sums[me]
    build_indices(levels, bands, samples, lower_ref, upper_ref, shift_ref, low_at, up_at, time_at)
    for state in states:
        state[pl.ds(bands, ROWS)] = jnp.zeros((ROWS, samples), jnp.float32)

    def level(step, starts, size):
        places = []
        for start in starts:
            places += places_of(step, start, size)
        merge_rows(step, places, states[step - 1], states[step], low_at, up_at, time_at)

    local = rows_each.bit_length() - 1
    group = chan_count * rows_each
    for c in range(chan_count):
        for b in range(beam_count):
            if (c, b) != (0, 0):
                copies[c, b].wait_recv()
        chan_from = xor(chan, chan_flips, c)
        where = pl.multiple_of(chan_from * rows_each, rows_each)
        places = []
        values = []
        for b in range(beam_count):
            for piece in range(0, rows_each, ROWS):
                places.append(b * group + where + piece)
                values.append(got[b * chan_count + chan_from, pl.ds(piece, ROWS)])
        for step in range(min(3, local)):
            rows = [pl.ds(place, ROWS) for place in places]
            whens = [time_at[step, at] for at in rows]
            uppers = [take(v, up_at[step, at], 0) for v, at in zip(values, rows)]
            uppers = [take(v, when & (samples - 1), 1) for v, when in zip(uppers, whens)]
            lowers = [take(v, low_at[step, at], 0) for v, at in zip(values, rows)]
            values = [v + jnp.where(when >= 0, u, 0.0) for v, u, when in zip(lowers, uppers, whens)]
        for place, value in zip(places, values):
            states[2][pl.ds(place, ROWS)] = value
        for step in range(3, local):
            level(step, [b * group + where for b in range(beam_count)], rows_each)
        depth = 0
        while (c + 1) % (2 << depth) == 0 and (2 << depth) <= chan_count:
            size = rows_each * (2 << depth)
            first = chan_from // (2 << depth) * size
            first = pl.multiple_of(first, size)
            level(local + depth, [b * group + first for b in range(beam_count)], size)
            depth += 1
    for step in range(local + chan_count.bit_length() - 1, levels):
        level(step, [0], bands)
    for c, b in turns:
        copies[c, b].wait_send()
    scores(states[levels - 1], widths_ref, limit_ref, out_ref, bands, samples, 256)


def shards(intensities, lower_index, upper_index, delay_shift, widths, max_delay):
    beam_count = lax.axis_size("beam")
    chan_count = lax.axis_size("chan")
    count = beam_count * chan_count
    beams, channels, samples = intensities.shape
    rows_each = channels // SUB0
    bands = count * rows_each
    levels = lower_index.shape[0]
    anywhere = pl.BlockSpec(memory_space=pl.ANY)
    return pl.pallas_call(
        functools.partial(kernel, beam_count, chan_count, levels),
        out_shape=jax.ShapeDtypeStruct((1, widths.shape[0], bands), jnp.float32),
        in_specs=[anywhere] * 6,
        out_specs=pl.BlockSpec(memory_space=pltpu.VMEM),
        scratch_shapes=[
            pltpu.VMEM((beams, channels, samples), intensities.dtype),
            pltpu.VMEM(lower_index.shape, jnp.int32),
            pltpu.VMEM(upper_index.shape, jnp.int32),
            pltpu.VMEM(delay_shift.shape, jnp.int32),
            pltpu.SMEM(widths.shape, jnp.int32),
            pltpu.SMEM(max_delay.shape, jnp.int32),
            pltpu.VMEM((count, rows_each, samples), jnp.float32),
            pltpu.VMEM((count, rows_each, samples), jnp.float32),
        ]
        + [pltpu.VMEM((bands + ROWS, samples), jnp.float32)] * levels
        + [pltpu.VMEM((levels, bands, samples), jnp.int32)] * 3
        + [
            pltpu.SemaphoreType.DMA((CHUNKS + 5,)),
            pltpu.SemaphoreType.DMA((count,)),
            pltpu.SemaphoreType.DMA((count,)),
        ],
        compiler_params=pltpu.CompilerParams(
            collective_id=0, has_side_effects=True, vmem_limit_bytes=56 * 1024 * 1024
        ),
        name="search",
    )(intensities, lower_index, upper_index, delay_shift, widths, max_delay)


def solution(mesh):
    in_specs = (P(None, ("beam", "chan"), None), P(), P(), P(), P(), P(("beam", "chan")))
    out_specs = P(("beam", "chan"), None, None)
    return jax.shard_map(shards, mesh=mesh, in_specs=in_specs, out_specs=out_specs, check_vma=False)
```

time: 49 us -> 28.6 us (0.58)
  Pallas kernels: 42.7 us -> 26.4 us
  local copies, waits for them, and re-layouts: 5.37 us -> 1.38 us
    pallas_call x1, Pallas kernels: 42.7 us -> 26.4 us  [shards(): pl.pallas_call(functools.partial(kernel, beam_count, chan_count, levels),...]
    unnamed x11 -> x1, local copies, waits for them, and re-layouts: 5.37 us -> 1.38 us
where the time goes in v1:
time: 28.6 us; the launch traced here: 28.4 us
  Pallas kernels  26.4 us (92%)
  local copies, waits for them, and re-layouts  1.38 us (5%)
  between operations  0.66 us (2%)
    pallas_call x1, Pallas kernels, shards(): pl.pallas_call(functools.partial(kernel, beam_count, chan_count, levels),...  26.4 us
    unnamed x1, local copies, waits for them, and re-layouts  1.38 us

profile of v1, /device:TPU:0, one launch (start us, length us, event | category | flops | bytes accessed | tf_op | source)
XLA Modules:
  0.0 28.4 jit_solution(9244285649472297049)
XLA Ops:
  0.7 26.4 %search.1 = f32[1,8,1024]{2,1,0:T(8,128)} custom-call(bf16[32,256,128]{2,1,0:T(8,128)(2,1)} %x_hbm.1, s32[10,1024]{1,0:T(8,128)} %lower_hbm.1, s32[10,1024]{1,0:T(8,128)} %upper_hbm.1, s32[10,1024]{1,0:T(8,128)} %shift_hbm.1, s32[8]{0:T(128)} %widths_hbm.1, s32[1]{0:T(128)S(6)} %copy.8.limit_hbm), custom_call_target="tpu_custom_call" | custom-call | tf_op jit(solution)/shard_map/search/pallas_call | solution.py:243
  27.0 1.4 %copy.9 = f32[1,8,1024]{2,1,0:T(8,128)} copy(f32[1,8,1024]{2,1,0:T(8,128)} %search.1) | data formatting | bytes 65536

commit v2 on v1

--- a/solution.py
+++ b/solution.py
@@ -134,7 +134,7 @@
                 value = value + step
         return value
 
-    turns = [(c, b) for c in reversed(range(chan_count)) for b in range(beam_count) if (c, b) != (0, 0)]
+    turns = [(c, b) for c in range(chan_count) for b in range(beam_count) if (c, b) != (0, 0)]
 
     def partner(c, b):
         return xor(beam, beam_flips, b), xor(chan, chan_flips, c)

time: 28.6 us -> 25.3 us (0.88)
  Pallas kernels: 26.4 us -> 22.9 us
    pallas_call x1, Pallas kernels: 26.4 us -> 22.9 us  [shards(): pl.pallas_call(functools.partial(kernel, beam_count, chan_count, levels),...]
where the time goes in v2:
time: 25.3 us; the launch traced here: 24.9 us
  Pallas kernels  22.9 us (91%)
  local copies, waits for them, and re-layouts  1.38 us (5%)
  between operations  0.66 us (3%)
    pallas_call x1, Pallas kernels, shards(): pl.pallas_call(functools.partial(kernel, beam_count, chan_count, levels),...  22.9 us
    unnamed x1, local copies, waits for them, and re-layouts  1.38 us

profile of v2, /device:TPU:0, one launch (start us, length us, event | category | flops | bytes accessed | tf_op | source)
XLA Modules:
  0.0 24.9 jit_solution(14922412549974290146)
XLA Ops:
  0.7 22.9 %search.1 = f32[1,8,1024]{2,1,0:T(8,128)} custom-call(bf16[32,256,128]{2,1,0:T(8,128)(2,1)} %x_hbm.1, s32[10,1024]{1,0:T(8,128)} %lower_hbm.1, s32[10,1024]{1,0:T(8,128)} %upper_hbm.1, s32[10,1024]{1,0:T(8,128)} %shift_hbm.1, s32[8]{0:T(128)} %widths_hbm.1, s32[1]{0:T(128)S(6)} %copy.8.limit_hbm), custom_call_target="tpu_custom_call" | custom-call | tf_op jit(solution)/shard_map/search/pallas_call | solution.py:243
  23.6 1.4 %copy.9 = f32[1,8,1024]{2,1,0:T(8,128)} copy(f32[1,8,1024]{2,1,0:T(8,128)} %search.1) | data formatting | bytes 65536

commit v3 on v2

--- a/solution.py
+++ b/solution.py
@@ -155,7 +155,7 @@
     ]
     for load in loads + tables:
         load.start()
-    for c, b in turns:
+    for c, b in reversed(turns):
         pl.semaphore_signal(barrier, inc=1, device_id=partner(c, b), device_id_type=MESH)
 
     band = lax.broadcasted_iota(jnp.int32, (rows_each, channels), 0)
@@ -226,9 +226,9 @@
             depth += 1
     for step in range(local + chan_count.bit_length() - 1, levels):
         level(step, [0], bands)
+    scores(states[levels - 1], widths_ref, limit_ref, out_ref, bands, samples, 256)
     for c, b in turns:
         copies[c, b].wait_send()
-    scores(states[levels - 1], widths_ref, limit_ref, out_ref, bands, samples, 256)
 
 
 def shards(intensities, lower_index, upper_index, delay_shift, widths, max_delay):

time: 25.3 us -> 24.8 us (0.980)
  Pallas kernels: 22.9 us -> 22.4 us
    pallas_call x1, Pallas kernels: 22.9 us -> 22.4 us  [shards(): pl.pallas_call(functools.partial(kernel, beam_count, chan_count, levels),...]
where the time goes in v3:
time: 24.8 us; the launch traced here: 24.5 us
  Pallas kernels  22.4 us (90%)
  local copies, waits for them, and re-layouts  1.38 us (6%)
  between operations  0.66 us (3%)
    pallas_call x1, Pallas kernels, shards(): pl.pallas_call(functools.partial(kernel, beam_count, chan_count, levels),...  22.4 us
    unnamed x1, local copies, waits for them, and re-layouts  1.38 us

profile of v3, /device:TPU:0, one launch (start us, length us, event | category | flops | bytes accessed | tf_op | source)
XLA Modules:
  0.0 24.5 jit_solution(8833528473807428063)
XLA Ops:
  0.7 22.4 %search.1 = f32[1,8,1024]{2,1,0:T(8,128)} custom-call(bf16[32,256,128]{2,1,0:T(8,128)(2,1)} %x_hbm.1, s32[10,1024]{1,0:T(8,128)} %lower_hbm.1, s32[10,1024]{1,0:T(8,128)} %upper_hbm.1, s32[10,1024]{1,0:T(8,128)} %shift_hbm.1, s32[8]{0:T(128)} %widths_hbm.1, s32[1]{0:T(128)S(6)} %copy.8.limit_hbm), custom_call_target="tpu_custom_call" | custom-call | tf_op jit(solution)/shard_map/search/pallas_call | solution.py:243
  23.1 1.4 %copy.9 = f32[1,8,1024]{2,1,0:T(8,128)} copy(f32[1,8,1024]{2,1,0:T(8,128)} %search.1) | data formatting | bytes 65536
